TPU v7x, 32 devices: a whole 2x2x4 slice. The times are simulated.
32 devices in a mesh: dp: 8 (over z, x), expert: 4 (over y, core).
Axes of the slice: x: 2, y: 2, z: 4, core: 2. Of those that a mesh axis runs over, the one named last changes fastest.
Arguments:
- layer_in: bfloat16 [8192, 1024], P(('dp', 'expert')), may hold values from -6 to 6
- body_of: int32 [8192], P(('dp', 'expert')), may hold values from 0 to 5, as said below
- expert_of: int32 [8192, 1], P(('dp', 'expert')), may hold values from 0 to 7; in each aligned block of 256 rows (0 to 255, 256 to 511, ...) at most 48 rows name the same one
- w_qkv: bfloat16 [1024, 1536], replicated, may hold values from -0.1875 to 0.1875
- w_o: bfloat16 [1024, 512], replicated, may hold values from -0.25 to 0.25
- w_up: bfloat16 [8, 1024, 1024], P('expert', None, 'dp'), may hold values from -0.1875 to 0.1875
- w_down: bfloat16 [8, 1024, 1024], P('expert', 'dp'), may hold values from -0.1875 to 0.1875
- d_out: bfloat16 [8192, 1024], P(('dp', 'expert')), may hold values from -6 to 6
Outputs:
- out: bfloat16 [8192, 1024], P(('dp', 'expert'))
- grad_input: bfloat16 [8192, 1024], P(('dp', 'expert'))
- grad_qkv: float32 [1024, 1536], P(('dp', 'expert'))
- grad_o: float32 [1024, 512], P(('dp', 'expert'))
- grad_up: float32 [8, 1024, 1024], P('expert', None, 'dp')
- grad_down: float32 [8, 1024, 1024], P('expert', 'dp')
Inputs may be any that keep to these rules, and one draw needn't show every extreme that they name: `body_of`: within each device's 256 rows the ids start at 0 and rise by one at each new body; every body has 16 to 128 tokens, no body crosses a multiple of 128 rows of its device, no block of 128 rows holds more than 3 bodies, and some device holds 3 bodies in each of its blocks. `expert_of`: in the 256 rows of one device no expert is named more than 48 times, a bound that some block reaches.
All inputs are finite; a program needn't handle non-finite values.
Results may differ from a plain program's by a relative error of at most 0.014.
Values may be sent and summed in bfloat16 or wider, within the bound.
A program may use at most 128 MiB of HBM per device.

v0:
```python
import jax
import jax.numpy as jnp
from jax import lax
from jax.sharding import PartitionSpec as P

HD = 64
EPSILON = 1e-06


def rms_norm(values):
    scale = lax.rsqrt(jnp.mean(values * values, axis=-1, keepdims=True) + EPSILON)
    return (values * scale).astype(jnp.bfloat16)


def gelu_tanh(values):
    return jax.nn.gelu(values, approximate=True)


def gelu_back(pre_act, cotangent):
    return jax.vjp(gelu_tanh, pre_act)[1](cotangent)[0]


def row_contract(left, right):
    return lax.dot_general(
        left, right, (((0,), (0,)), ((), ())), preferred_element_type=jnp.float32
    )


def col_contract(left, right):
    return lax.dot_general(
        left, right, (((1,), (1,)), ((), ())), preferred_element_type=jnp.float32
    )


def attention_core(packed, labels_row):
    rows = packed.shape[0]
    blocks = rows // 128
    width = packed.shape[1] // 3
    heads = width // HD
    parts = packed.reshape(blocks, 128, 3, heads, HD)
    query = parts[:, :, 0]
    keys = parts[:, :, 1]
    values = parts[:, :, 2]
    scores = jnp.einsum(
        "bqhc,bkhc->bhqk", query, keys, preferred_element_type=jnp.float32
    ) * HD ** (-0.5)
    labels = labels_row.reshape(blocks, 128)
    same = (labels[:, :, None] == labels[:, None, :])[:, None]
    weights = jnp.where(same, jnp.exp(scores), 0.0)
    probs = (weights / jnp.sum(weights, axis=-1, keepdims=True)).astype(jnp.bfloat16)
    mixed = jnp.einsum("bhqk,bkhc->bqhc", probs, values, preferred_element_type=jnp.float32)
    return mixed.astype(jnp.bfloat16).reshape(rows, width)


def on_device(layer_in, body_of, expert_of, w_qkv, w_o, w_up, w_down, d_out):
    tok_rows = layer_in.shape[0]
    width = layer_in.shape[1]
    shards = lax.axis_size("expert")
    local_experts = w_up.shape[0]
    all_experts = local_experts * shards
    capacity = 3 * tok_rows // (2 * all_experts)
    received = shards * capacity
    layer_f = layer_in.astype(jnp.float32)
    normed, norm_x_back = jax.vjp(rms_norm, layer_f)
    packed = jnp.dot(normed, w_qkv, preferred_element_type=jnp.float32).astype(jnp.bfloat16)
    mixed, core_back = jax.vjp(lambda value: attention_core(value, body_of), packed)
    resid = (layer_f + col_contract(mixed, w_o)).astype(jnp.bfloat16)
    inner, norm_h_back = jax.vjp(rms_norm, resid.astype(jnp.float32))
    expert_ids = expert_of[:, 0]
    onehot = (expert_ids[:, None] == jnp.arange(all_experts, dtype=jnp.int32)[None, :]).astype(
        jnp.int32
    )
    ranks = jnp.sum(jnp.cumsum(onehot, axis=0) * onehot, axis=-1) - 1
    slots = expert_ids * capacity + ranks

    def to_slots(values):
        store = jnp.zeros((all_experts * capacity, width), values.dtype).at[slots].set(values)
        return store.reshape(shards, local_experts, capacity, width)

    sent_inner = lax.all_to_all(to_slots(inner), "expert", split_axis=0, concat_axis=2, tiled=True)
    inputs = sent_inner.reshape(local_experts, received, width)
    full_up, full_down = (
        lax.all_gather(w_up, "dp", axis=2, tiled=True),
        lax.all_gather(w_down, "dp", axis=1, tiled=True),
    )
    pre_act = jnp.einsum("esd,edf->esf", inputs, full_up, preferred_element_type=jnp.float32)
    hidden = gelu_tanh(pre_act).astype(jnp.bfloat16)
    result = jnp.einsum("esf,efd->esd", hidden, full_down, preferred_element_type=jnp.float32)
    outgoing = result.astype(jnp.bfloat16).reshape(1, local_experts, received, width)
    returned = lax.all_to_all(outgoing, "expert", split_axis=2, concat_axis=0, tiled=True)
    expert_out = returned.reshape(all_experts * capacity, width)[slots]
    out = (resid.astype(jnp.float32) + expert_out.astype(jnp.float32)).astype(jnp.bfloat16)
    sent_grads = lax.all_to_all(to_slots(d_out), "expert", split_axis=0, concat_axis=2, tiled=True)
    grads_in = sent_grads.reshape(local_experts, received, width)
    d_hidden = jnp.einsum("esd,efd->esf", grads_in, full_down, preferred_element_type=jnp.float32)
    d_pre = gelu_back(pre_act, d_hidden).astype(jnp.bfloat16)
    part_up = jnp.einsum("esd,esf->edf", inputs, d_pre, preferred_element_type=jnp.float32)
    part_down = jnp.einsum("esf,esd->efd", hidden, grads_in, preferred_element_type=jnp.float32)
    d_inputs = jnp.einsum("esf,edf->esd", d_pre, full_up, preferred_element_type=jnp.float32)
    going_back = d_inputs.astype(jnp.bfloat16).reshape(1, local_experts, received, width)
    came_back = lax.all_to_all(going_back, "expert", split_axis=2, concat_axis=0, tiled=True)
    d_inner = came_back.reshape(all_experts * capacity, width)[slots]
    grad_up, grad_down = (
        lax.psum_scatter(
            part_up.astype(jnp.bfloat16), "dp", scatter_dimension=2, tiled=True
        ).astype(jnp.float32),
        lax.psum_scatter(
            part_down.astype(jnp.bfloat16), "dp", scatter_dimension=1, tiled=True
        ).astype(jnp.float32),
    )
    d_resid = (d_out.astype(jnp.float32) + norm_h_back(d_inner)[0]).astype(jnp.bfloat16)
    term_o = row_contract(d_resid, mixed)
    d_mixed = jnp.dot(d_resid, w_o, preferred_element_type=jnp.float32).astype(jnp.bfloat16)
    d_packed = core_back(d_mixed)[0]
    term_qkv = row_contract(normed, d_packed)
    grad_qkv, grad_o = (
        lax.psum_scatter(term_qkv, ("dp", "expert"), scatter_dimension=0, tiled=True),
        lax.psum_scatter(term_o, ("dp", "expert"), scatter_dimension=0, tiled=True),
    )
    d_normed = col_contract(d_packed, w_qkv).astype(jnp.bfloat16)
    grad_input = (d_resid.astype(jnp.float32) + norm_x_back(d_normed)[0]).astype(jnp.bfloat16)
    return (out, grad_input, grad_qkv, grad_o, grad_up, grad_down)


def solution(mesh):
    in_specs = (
        P(("dp", "expert"), None),
        P(("dp", "expert")),
        P(("dp", "expert"), None),
        P(),
        P(),
        P("expert", None, "dp"),
        P("expert", "dp", None),
        P(("dp", "expert"), None),
    )
    out_specs = (
        P(("dp", "expert"), None),
        P(("dp", "expert"), None),
        P(("dp", "expert"), None),
        P(("dp", "expert"), None),
        P("expert", None, "dp"),
        P("expert", "dp", None),
    )
    return jax.shard_map(
        on_device, mesh=mesh, in_specs=in_specs, out_specs=out_specs, check_vma=False
    )
```

profile of v0, /device:TPU:0, one launch (start us, length us, event | category | flops | bytes accessed | tf_op | source)
XLA Modules:
  0.0 630.3 jit_solution(3287069089571837965)
XLA Ops:
  7.2 0.7 all-gather.5.cloned.1.call-update
  8.0 0.7 all-gather.3.cloned.1.call-update
  8.7 0.7 fusion.59
  10.2 0.8 fusion.58
  11.0 0.7 compare_select_fusion
  11.6 3.1 scatter_custom_fusion.1
  14.7 4.2 all-to-all-start.2
  19.0 1.3 fusion.25
  20.2 3.0 convolution_convert_fusion.2
  23.2 3.1 reshape.172
  26.4 2.5 fusion.64
  28.9 2.0 copy.70
  30.9 2.0 copy.69
  32.9 1.3 copy.68
  34.4 1.5 select_reduce_fusion
  36.0 0.8 copy-done.6
  37.8 1.3 fusion.28
  39.1 3.2 scatter_custom_fusion
  42.3 4.2 all-to-all-start
  46.8 2.1 copy.50
  48.9 9.9 %all-to-all-done = bf16[4,2,48,1024]{3,2,1,0:T(8,128)(2,1)} async-done(((bf16[4,2,48,1024]{3,2,1,0:T(8,128)(2,1)}), bf16[4,2,48,1024]{3,2,1,0:T(8,128)(2,1)}, u32[]{:S(2)}, u32[]{:S(2)}) %all-to-all-start) | async-done | bytes 786464 | tf_op jit(solution)/shard_map/all_to_all | solution.py:80
  58.8 2.1 copy.47
  60.9 25.4 %all-gather.5.cloned.1.call-done = bf16[2,1024,1024]{2,1,0:T(8,128)(2,1)} async-done(((bf16[2,128,1024]{2,1,0:T(8,128)(2,1)}), bf16[2,1024,1024]{2,1,0:T(8,128)(2,1)}) %all-gather.5.cloned.1.call-update) | async-done | bytes 4194320 | tf_op jit(solution)/shard_map/all_gather | solution.py:84
  86.3 5.1 fusion.65
  91.4 70.3 %all-gather.3.cloned.1.call-done = bf16[2,1024,1024]{2,1,0:T(8,128)(2,1)} async-done(((bf16[2,1024,128]{2,1,0:T(8,128)(2,1)}), bf16[2,1024,1024]{2,1,0:T(8,128)(2,1)}) %all-gather.3.cloned.1.call-update) | async-done | bytes 4194320 | tf_op jit(solution)/shard_map/all_gather | solution.py:83
  161.7 6.0 fusion.6
  167.6 0.9 copy-done.11
  168.5 3.2 convolution_convert_fusion.1
  171.7 11.3 %copy.64 = bf16[2,1024,1024]{1,0,2:T(2,128)(2,1)} copy(bf16[2,1024,1024]{2,1,0:T(8,128)(2,1)} %convolution_convert_fusion.1) | data formatting | bytes 8388608
  183.1 5.6 copy.73
  188.7 4.9 convolution_convert_fusion
  193.6 4.1 fusion.9
  197.7 1.7 copy.51
  199.4 4.2 all-to-all-start.3
  203.6 3.9 fusion.8
  207.5 1.7 copy.48
  209.2 6.1 all-to-all-done.3
  215.3 4.2 all-to-all-start.1
  219.8 2.2 copy.52
  222.0 9.2 %all-to-all-done.1 = bf16[1,2,192,1024]{3,1,0,2:T(2,128)(2,1)} async-done(((bf16[1,2,192,1024]{3,1,0,2:T(2,128)(2,1)}), bf16[1,2,192,1024]{3,1,0,2:T(2,128)(2,1)}, u32[]{:S(2)}, u32[]{:S(2)}) %all-to-all-start.1) | async-done | bytes 786464 | tf_op jit(solution)/shard_map/all_to_all | solution.py:90
  231.3 2.2 copy.49
  233.5 3.6 gather_fusion.1
  237.1 3.6 gather_fusion
  240.7 1.4 fusion.31
  242.1 2.8 fusion.22
  244.9 0.8 copy-done.1
  245.7 1.9 fusion.43
  247.6 2.5 convolution_convert_fusion.10
  250.2 1.8 copy.53
  252.0 1.7 reshape.136
  253.7 2.2 fusion.20
  257.9 0.8 copy.59
  258.7 0.9 copy-done.12
  259.6 3.8 fusion.32
  263.4 2.5 fusion.27
  265.9 1.2 fusion.24
  267.1 7.8 %reduce-scatter.13.cloned.1.call-done = bf16[128,2048]{1,0:T(8,128)(2,1)} async-done(((bf16[1024,2048]{1,0:T(8,128)(2,1)}), bf16[128,2048]{1,0:T(8,128)(2,1)}) %reduce-scatter.13.cloned.1.call-update) | async-done | bytes 524304
  274.9 2.2 reshape.171
  277.1 2.0 copy.65
  279.1 2.1 convert_element_type.145
  281.2 85.5 %reduce-scatter.11.cloned.1.call-done = bf16[2,128,1024]{2,1,0:T(8,128)(2,1)} async-done(((bf16[2,1024,1024]{2,1,0:T(8,128)(2,1)}), bf16[2,128,1024]{2,1,0:T(8,128)(2,1)}) %reduce-scatter.11.cloned.1.call-update) | async-done | bytes 524304 | tf_op jit(solution)/shard_map/reduce_scatter | solution.py:107
  366.7 2.1 convert_element_type.147
  368.8 137.2 %reduce-scatter.9.cloned.1.call-done = f32[32,512]{1,0:T(8,128)} async-done(((f32[1024,512]{1,0:T(8,128)}), f32[32,512]{1,0:T(8,128)}) %reduce-scatter.9.cloned.1.call-update) | async-done | bytes 65552 | tf_op jit(solution)/shard_map/reduce_scatter | solution.py:118
  506.0 117.4 %reduce-scatter.7.cloned.1.call-done = f32[32,1536]{1,0:T(8,128)} async-done(((f32[1024,1536]{1,0:T(8,128)}), f32[32,1536]{1,0:T(8,128)}) %reduce-scatter.7.cloned.1.call-update) | async-done | bytes 196624 | tf_op jit(solution)/shard_map/reduce_scatter | solution.py:117
  (67 shorter events, 4.8 us)
Async XLA Ops:
  7.2 13.1 %copy-start = (bf16[1024,1536]{1,0:T(8,128)(2,1)S(1)}, bf16[1024,1536]{1,0:T(8,128)(2,1)}, u32[]{:S(2)}) copy-start(bf16[1024,1536]{1,0:T(8,128)(2,1)} %param.11) | copy-start | bytes 9437188
  7.2 79.1 %all-gather.5.cloned.1.call-start = ((), (), s32[]{:S(2)}) async-start(), calls=%async_computation.9 | async-start | bytes 4718592 | tf_op jit(solution)/shard_map/all_gather | solution.py:84
  7.9 153.8 %all-gather.3.cloned.1.call-start = ((), (), s32[]{:S(2)}) async-start(), calls=%async_computation.8 | async-start | bytes 4718592 | tf_op jit(solution)/shard_map/all_gather | solution.py:83
  14.7 27.6 %all-to-all-start.2 = ((bf16[4,2,48,1024]{3,2,1,0:T(8,128)(2,1)}), bf16[4,2,48,1024]{3,2,1,0:T(8,128)(2,1)}, u32[]{:S(2)}, u32[]{:S(2)}) async-start(bf16[4,2,48,1024]{3,2,1,0:T(8,128)(2,1)} %bitcast.121), calls=%async_computation.2 | async-start | bytes 1572864 | tf_op jit(solution)/shard_map/all_to_all | solution.py:93
  28.9 5.4 copy-start.19
  35.8 1.5 copy-start.8
  35.8 1.5 copy-start.3
  35.9 1.9 copy-start.14
  36.0 0.8 copy-start.6
  37.4 1.7 copy-start.15
  42.3 16.5 %all-to-all-start = ((bf16[4,2,48,1024]{3,2,1,0:T(8,128)(2,1)}), bf16[4,2,48,1024]{3,2,1,0:T(8,128)(2,1)}, u32[]{:S(2)}, u32[]{:S(2)}) async-start(bf16[4,2,48,1024]{3,2,1,0:T(8,128)(2,1)} %bitcast.122), calls=%async_computation | async-start | bytes 1572864 | tf_op jit(solution)/shard_map/all_to_all | solution.py:80
  46.5 228.4 %reduce-scatter.13.cloned.1.call-start = ((), (), s32[]{:S(2)}) async-start(), calls=%async_computation.13 | async-start | bytes 4718592
  161.7 6.8 %copy-start.10 = (bf16[1,2,4,48,1024]{4,3,2,1,0:T(8,128)(2,1)S(1)}, bf16[1,2,4,48,1024]{4,3,2,1,0:T(8,128)(2,1)}, u32[]{:S(2)}) copy-start(bf16[1,2,4,48,1024]{4,3,2,1,0:T(8,128)(2,1)} %copy.47) | copy-start | bytes 2359300
  167.6 0.9 copy-start.11
  188.6 178.1 %reduce-scatter.11.cloned.1.call-start = ((), (), s32[]{:S(2)}) async-start(), calls=%async_computation.12 | async-start | bytes 4718592 | tf_op jit(solution)/shard_map/reduce_scatter | solution.py:107
  199.4 15.9 %all-to-all-start.3 = ((bf16[1,2,192,1024]{3,1,0,2:T(2,128)(2,1)}), bf16[1,2,192,1024]{3,1,0,2:T(2,128)(2,1)}, u32[]{:S(2)}, u32[]{:S(2)}) async-start(bf16[1,2,192,1024]{3,1,0,2:T(2,128)(2,1)} %copy.51), calls=%async_computation.3 | async-start | bytes 1572864 | tf_op jit(solution)/shard_map/all_to_all | solution.py:101
  215.3 15.9 %all-to-all-start.1 = ((bf16[1,2,192,1024]{3,1,0,2:T(2,128)(2,1)}), bf16[1,2,192,1024]{3,1,0,2:T(2,128)(2,1)}, u32[]{:S(2)}, u32[]{:S(2)}) async-start(bf16[1,2,192,1024]{3,1,0,2:T(2,128)(2,1)} %copy.48), calls=%async_computation.1 | async-start | bytes 1572864 | tf_op jit(solution)/shard_map/all_to_all | solution.py:90
  219.5 286.5 %reduce-scatter.9.cloned.1.call-start = ((), (), s32[]{:S(2)}) async-start(), calls=%async_computation.11 | async-start | bytes 2162688 | tf_op jit(solution)/shard_map/reduce_scatter | solution.py:118
  242.1 3.6 copy-start.16
  244.9 0.8 copy-start.1
  247.6 375.9 %reduce-scatter.7.cloned.1.call-start = ((), (), s32[]{:S(2)}) async-start(), calls=%async_computation.10 | async-start | bytes 6488064 | tf_op jit(solution)/shard_map/reduce_scatter | solution.py:117
  253.7 2.2 copy-start.7
  253.7 2.2 copy-start.13
  253.7 2.7 copy-start.9
  253.7 2.7 copy-start.17
  256.4 1.0 copy-start.18
  257.8 1.8 copy-start.4
  258.7 0.9 copy-start.12
  263.4 2.5 copy-start.2
  263.4 2.5 copy-start.5
Sparse Core Ops, SparseCore 0:
  10.2 76.0 all-gather.4
  88.3 73.2 all-gather.2
  188.8 86.0 reduce-scatter.12
  278.8 87.8 reduce-scatter.10
  369.4 136.5 reduce-scatter.8
  513.0 110.3 reduce-scatter.6
where the time goes:
time: 632 us; the launch traced here: 630 us
  waiting for transfers between devices  470 us (74%)
  local copies, waits for them, and re-layouts  63.7 us (10%)
  matrix products  47.3 us (7%)
  starting transfers between devices  17.5 us (3%)
  other arithmetic  17.1 us (3%)
  between operations  14.5 us (2%)
    reduce_scatter x1, waiting for transfers between devices, on_device(): lax.psum_scatter(term_o, ('dp', 'expert'), scatter_dimension=0, tiled=True)  137 us
    reduce_scatter x1, waiting for transfers between devices, on_device(): lax.psum_scatter(term_qkv, ('dp', 'expert'), scatter_dimension=0, tiled=T...  117 us
    reduce_scatter x1, waiting for transfers between devices, on_device(): lax.psum_scatter(part_down.astype(jnp.bfloat16), 'dp', scatter_dimension=...  85.5 us
    all_gather x1, waiting for transfers between devices, on_device(): lax.all_gather(w_up, 'dp', axis=2, tiled=True)  70.3 us
    unnamed x47, local copies, waits for them, and re-layouts  30.8 us
    all_gather x1, waiting for transfers between devices, on_device(): lax.all_gather(w_down, 'dp', axis=1, tiled=True)  25.4 us
  transfers between devices with their start and end apart: 10, of which 9 were waited for; matrix products, arithmetic and copies ran while one was open for 16% of the time, Pallas kernels for 0%

commit v1 on v0

--- a/solution.py
+++ b/solution.py
@@ -1,3 +1,4 @@
+import functools
 import jax
 import jax.numpy as jnp
 from jax import lax
@@ -5,6 +6,24 @@
 
 HD = 64
 EPSILON = 1e-06
+
+
+def obtain_runs(u_in, row_axis):
+    block_now = lax.axis_size(row_axis)
+    carry = lax.axis_index(row_axis)
+    newest, g_now = (block_now, carry)
+    x_next, a_next = (u_in, 1)
+    while a_next < newest:
+        frame_out = tuple(((dev_j, dev_j ^ a_next) for dev_j in range(newest)))
+        reached = lax.ppermute(x_next, row_axis, perm=frame_out)
+        high = jnp.concatenate([x_next, reached], axis=2)
+        h_now = jnp.concatenate([reached, x_next], 2)
+        x_next = jnp.where(g_now & a_next == 0, high, h_now)
+        a_next = 2 * a_next
+    return x_next
+
+
+launch_the_orders = functools.partial(obtain_runs, row_axis="dp")
 
 
 def rms_norm(values):
@@ -79,10 +98,7 @@
 
     sent_inner = lax.all_to_all(to_slots(inner), "expert", split_axis=0, concat_axis=2, tiled=True)
     inputs = sent_inner.reshape(local_experts, received, width)
-    full_up, full_down = (
-        lax.all_gather(w_up, "dp", axis=2, tiled=True),
-        lax.all_gather(w_down, "dp", axis=1, tiled=True),
-    )
+    full_up, full_down = (launch_the_orders(w_up), lax.all_gather(w_down, "dp", axis=1, tiled=True))
     pre_act = jnp.einsum("esd,edf->esf", inputs, full_up, preferred_element_type=jnp.float32)
     hidden = gelu_tanh(pre_act).astype(jnp.bfloat16)
     result = jnp.einsum("esf,efd->esd", hidden, full_down, preferred_element_type=jnp.float32)

time: 632 us -> 657 us (1.040)
  waiting for transfers between devices: 470 us -> 484 us
  other arithmetic: 17.1 us -> 25.6 us
    ppermute x0 -> x3, waiting for transfers between devices: none -> 70.5 us  [obtain_runs(): reached = lax.ppermute(x_next, row_axis, perm=frame_out)]
    all_gather x1 -> x0, waiting for transfers between devices: 70.3 us -> none  [on_device(): lax.all_gather(w_up, 'dp', axis=2, tiled=True)]
    all_gather x1, waiting for transfers between devices: 25.4 us -> 41.5 us  [on_device(): lax.all_gather(w_down, 'dp', axis=1, tiled=True)]
    select_n x0 -> x2, other arithmetic: none -> 7.12 us  [obtain_runs(): x_next = jnp.where(g_now & a_next == 0, high, h_now)]
    unnamed x47 -> x51, local copies, waits for them, and re-layouts: 30.8 us -> 30 us
  transfers between devices with their start and end apart: 10 -> 12, of which waited for: 9 -> 11; matrix products, arithmetic and copies ran while one was open for 16% -> 16% of each run, Pallas kernels for 0% -> 0%
where the time goes in v1:
time: 657 us; the launch traced here: 655 us
  waiting for transfers between devices  484 us (74%)
  local copies, waits for them, and re-layouts  62.7 us (10%)
  matrix products  46.7 us (7%)
  other arithmetic  25.6 us (4%)
  starting transfers between devices  21.6 us (3%)
  between operations  14.1 us (2%)
    reduce_scatter x1, waiting for transfers between devices, on_device(): lax.psum_scatter(term_o, ('dp', 'expert'), scatter_dimension=0, tiled=True)  137 us
    reduce_scatter x1, waiting for transfers between devices, on_device(): lax.psum_scatter(term_qkv, ('dp', 'expert'), scatter_dimension=0, tiled=T...  117 us
    reduce_scatter x1, waiting for transfers between devices, on_device(): lax.psum_scatter(part_down.astype(jnp.bfloat16), 'dp', scatter_dimension=...  85.4 us
    ppermute x3, waiting for transfers between devices, obtain_runs(): reached = lax.ppermute(x_next, row_axis, perm=frame_out)  70.5 us
    all_gather x1, waiting for transfers between devices, on_device(): lax.all_gather(w_down, 'dp', axis=1, tiled=True)  41.5 us
    unnamed x51, local copies, waits for them, and re-layouts  30 us
  transfers between devices with their start and end apart: 12, of which 11 were waited for; matrix products, arithmetic and copies ran while one was open for 16% of the time, Pallas kernels for 0%

profile of v1, /device:TPU:0, one launch (start us, length us, event | category | flops | bytes accessed | tf_op | source)
XLA Modules:
  0.0 655.0 jit_solution(10105229117529455161)
XLA Ops:
  7.9 3.0 collective-permute-start
  13.9 3.1 scatter_custom_fusion.1
  17.0 4.2 all-to-all-start.2
  21.2 1.3 fusion.25
  22.5 1.3 collective-permute-done
  23.8 3.0 maximum_select_fusion.2
  26.8 1.3 collective-permute-start.1
  28.1 2.0 convolution_convert_fusion.2
  30.0 3.1 reshape.172
  33.1 2.5 fusion.67
  35.6 1.3 copy.70
  37.0 2.1 copy.69
  39.2 35.6 %collective-permute-done.1 = bf16[2,1024,256]{2,1,0:T(8,128)(2,1)} collective-permute-done((bf16[2,1024,256]{2,1,0:T(8,128)(2,1)}, bf16[2,1024,256]{2,1,0:T(8,128)(2,1)}, u32[]{:S(2)}, u32[]{:S(2)}) %collective-permute-start.1) | collective-permute-done | bytes 1048608 | tf_op jit(solution)/shard_map/ppermute | solution.py:18
  74.8 4.2 maximum_select_fusion.1
  79.0 1.4 select_reduce_fusion
  80.3 1.3 copy.68
  81.7 1.5 divide_convert_fusion
  84.6 1.3 fusion.28
  85.9 3.2 scatter_custom_fusion
  89.0 4.2 all-to-all-start
  93.5 2.1 copy.50
  95.5 9.4 %all-to-all-done = bf16[4,2,48,1024]{3,2,1,0:T(8,128)(2,1)} async-done(((bf16[4,2,48,1024]{3,2,1,0:T(8,128)(2,1)}), bf16[4,2,48,1024]{3,2,1,0:T(8,128)(2,1)}, u32[]{:S(2)}, u32[]{:S(2)}) %all-to-all-start) | async-done | bytes 786464 | tf_op jit(solution)/shard_map/all_to_all | solution.py:99
  104.9 2.1 copy.47
  107.0 41.5 %all-gather.2.cloned.1.call-done = bf16[2,1024,1024]{2,1,0:T(8,128)(2,1)} async-done(((bf16[2,128,1024]{2,1,0:T(8,128)(2,1)}), bf16[2,1024,1024]{2,1,0:T(8,128)(2,1)}) %all-gather.2.cloned.1.call-update) | async-done | bytes 4194320 | tf_op jit(solution)/shard_map/all_gather | solution.py:101
  148.5 4.0 fusion.68
  152.6 33.6 %collective-permute-done.2 = bf16[2,1024,512]{2,1,0:T(8,128)(2,1)} collective-permute-done((bf16[2,1024,512]{2,1,0:T(8,128)(2,1)}, bf16[2,1024,512]{2,1,0:T(8,128)(2,1)}, u32[]{:S(2)}, u32[]{:S(2)}) %collective-permute-start.2) | collective-permute-done | bytes 2097184 | tf_op jit(solution)/shard_map/ppermute | solution.py:18
  186.2 6.4 fusion.6
  192.6 0.9 copy-done.16
  193.5 3.4 convolution_convert_fusion.1
  196.9 11.3 %copy.64 = bf16[2,1024,1024]{1,0,2:T(2,128)(2,1)} copy(bf16[2,1024,1024]{2,1,0:T(8,128)(2,1)} %convolution_convert_fusion.1) | data formatting | bytes 8388608
  208.2 5.7 copy.73
  214.0 5.0 convolution_convert_fusion
  219.0 5.3 fusion.9
  224.3 1.7 copy.51
  226.0 4.2 all-to-all-start.3
  230.2 3.9 fusion.8
  234.1 1.7 copy.48
  235.8 6.1 all-to-all-done.3
  241.9 4.2 all-to-all-start.1
  246.4 2.2 copy.52
  248.6 9.2 %all-to-all-done.1 = bf16[1,2,192,1024]{3,1,0,2:T(2,128)(2,1)} async-done(((bf16[1,2,192,1024]{3,1,0,2:T(2,128)(2,1)}), bf16[1,2,192,1024]{3,1,0,2:T(2,128)(2,1)}, u32[]{:S(2)}, u32[]{:S(2)}) %all-to-all-start.1) | async-done | bytes 786464 | tf_op jit(solution)/shard_map/all_to_all | solution.py:106
  257.8 2.2 copy.49
  260.1 3.6 gather_fusion.1
  263.6 3.6 gather_fusion
  267.3 1.5 fusion.31
  268.7 2.7 fusion.22
  272.3 1.8 fusion.44
  274.2 2.5 convolution_convert_fusion.10
  276.7 1.8 copy.53
  278.5 1.7 reshape.136
  280.3 1.9 fusion.20
  284.2 0.8 copy.59
  285.0 0.9 copy-done.11
  285.9 3.7 fusion.32
  289.6 2.5 fusion.27
  292.1 1.2 fusion.24
  293.3 6.9 %reduce-scatter.13.cloned.1.call-done = bf16[128,2048]{1,0:T(8,128)(2,1)} async-done(((bf16[1024,2048]{1,0:T(8,128)(2,1)}), bf16[128,2048]{1,0:T(8,128)(2,1)}) %reduce-scatter.13.cloned.1.call-update) | async-done | bytes 524304
  300.2 2.2 reshape.171
  302.4 2.0 copy.65
  304.4 2.1 convert_element_type.145
  306.5 85.4 %reduce-scatter.11.cloned.1.call-done = bf16[2,128,1024]{2,1,0:T(8,128)(2,1)} async-done(((bf16[2,1024,1024]{2,1,0:T(8,128)(2,1)}), bf16[2,128,1024]{2,1,0:T(8,128)(2,1)}) %reduce-scatter.11.cloned.1.call-update) | async-done | bytes 524304 | tf_op jit(solution)/shard_map/reduce_scatter | solution.py:123
  391.9 2.1 convert_element_type.147
  394.1 137.2 %reduce-scatter.9.cloned.1.call-done = f32[32,512]{1,0:T(8,128)} async-done(((f32[1024,512]{1,0:T(8,128)}), f32[32,512]{1,0:T(8,128)}) %reduce-scatter.9.cloned.1.call-update) | async-done | bytes 65552 | tf_op jit(solution)/shard_map/reduce_scatter | solution.py:134
  531.2 117.3 %reduce-scatter.7.cloned.1.call-done = f32[32,1536]{1,0:T(8,128)} async-done(((f32[1024,1536]{1,0:T(8,128)}), f32[32,1536]{1,0:T(8,128)}) %reduce-scatter.7.cloned.1.call-update) | async-done | bytes 196624 | tf_op jit(solution)/shard_map/reduce_scatter | solution.py:133
  (76 shorter events, 8.6 us)
Async XLA Ops:
  7.2 20.9 %copy-start = (bf16[1024,1536]{1,0:T(8,128)(2,1)S(1)}, bf16[1024,1536]{1,0:T(8,128)(2,1)}, u32[]{:S(2)}) copy-start(bf16[1024,1536]{1,0:T(8,128)(2,1)} %param.11) | copy-start | bytes 9437188
  7.2 141.4 %all-gather.2.cloned.1.call-start = ((), (), s32[]{:S(2)}) async-start(), calls=%async_computation.8 | async-start | bytes 4718592 | tf_op jit(solution)/shard_map/all_gather | solution.py:101
  7.9 15.9 %collective-permute-start = (bf16[2,1024,128]{2,1,0:T(8,128)(2,1)}, bf16[2,1024,128]{2,1,0:T(8,128)(2,1)}, u32[]{:S(2)}, u32[]{:S(2)}) collective-permute-start(bf16[2,1024,128]{2,1,0:T(8,128)(2,1)} %param.13), channel_id=1, source_target_pairs={{0,4},{4,0},{8,12},{12,8},{16,20},{20,16},{24,28},{28,24},{1,5},{5... | collective-permute-start | bytes 1572872 | tf_op jit(solution)/shard_map/ppermute | solution.py:18
  17.0 72.0 %all-to-all-start.2 = ((bf16[4,2,48,1024]{3,2,1,0:T(8,128)(2,1)}), bf16[4,2,48,1024]{3,2,1,0:T(8,128)(2,1)}, u32[]{:S(2)}, u32[]{:S(2)}) async-start(bf16[4,2,48,1024]{3,2,1,0:T(8,128)(2,1)} %bitcast.119), calls=%async_computation.2 | async-start | bytes 1572864 | tf_op jit(solution)/shard_map/all_to_all | solution.py:109
  21.2 6.8 %copy-start.3 = (bf16[256,1024]{1,0:T(8,128)(2,1)S(1)}, bf16[256,1024]{1,0:T(8,128)(2,1)}, u32[]{:S(2)}) copy-start(bf16[256,1024]{1,0:T(8,128)(2,1)} %param.8) | copy-start | bytes 1572868
  26.8 48.0 %collective-permute-start.1 = (bf16[2,1024,256]{2,1,0:T(8,128)(2,1)}, bf16[2,1024,256]{2,1,0:T(8,128)(2,1)}, u32[]{:S(2)}, u32[]{:S(2)}) collective-permute-start(bf16[2,1024,256]{2,1,0:T(8,128)(2,1)} %maximum_select_fusion.2), channel_id=1, source_target_pairs={{0,8},{4,12},{8,0},{12,4},{16,24},{20,28},{24,16},{28,20},{1,9},{5... | collective-permute-start | bytes 3145736 | tf_op jit(solution)/shard_map/ppermute | solution.py:18
  33.1 6.0 copy-start.21
  37.0 42.0 %copy-start.17 = (bf16[2,128,1,8,64]{1,4,3,0,2:T(8,128)(2,1)}, bf16[2,128,1,8,64]{1,4,3,0,2:T(8,128)(2,1)S(1)}, u32[]{:S(2)}) copy-start(bf16[2,128,1,8,64]{1,4,3,0,2:T(8,128)(2,1)S(1)} %copy.70) | copy-start | bytes 786436
  39.2 39.7 %copy-start.19 = (bf16[2,128,1,8,64]{1,4,3,0,2:T(8,128)(2,1)S(1)}, bf16[2,128,1,8,64]{1,4,3,0,2:T(8,128)(2,1)}, u32[]{:S(2)}) copy-start(bf16[2,128,1,8,64]{1,4,3,0,2:T(8,128)(2,1)} %copy.69) | copy-start | bytes 786436
  78.9 107.3 %collective-permute-start.2 = (bf16[2,1024,512]{2,1,0:T(8,128)(2,1)}, bf16[2,1024,512]{2,1,0:T(8,128)(2,1)}, u32[]{:S(2)}, u32[]{:S(2)}) collective-permute-start(bf16[2,1024,512]{2,1,0:T(8,128)(2,1)} %maximum_select_fusion.1), channel_id=1, source_target_pairs={{0,16},{4,20},{8,24},{12,28},{16,0},{20,4},{24,8},{28,12},{1,17},{... | collective-permute-start | bytes 6291464 | tf_op jit(solution)/shard_map/ppermute | solution.py:18
  81.7 2.9 copy-start.4
  81.7 2.9 copy-start.13
  83.2 0.8 copy-start.7
  84.5 1.3 copy-start.14
  89.0 15.9 %all-to-all-start = ((bf16[4,2,48,1024]{3,2,1,0:T(8,128)(2,1)}), bf16[4,2,48,1024]{3,2,1,0:T(8,128)(2,1)}, u32[]{:S(2)}, u32[]{:S(2)}) async-start(bf16[4,2,48,1024]{3,2,1,0:T(8,128)(2,1)} %bitcast.120), calls=%async_computation | async-start | bytes 1572864 | tf_op jit(solution)/shard_map/all_to_all | solution.py:99
  93.2 207.0 %reduce-scatter.13.cloned.1.call-start = ((), (), s32[]{:S(2)}) async-start(), calls=%async_computation.12 | async-start | bytes 4718592
  148.5 37.7 %copy-start.10 = (bf16[1,2,4,48,1024]{4,3,2,1,0:T(8,128)(2,1)S(1)}, bf16[1,2,4,48,1024]{4,3,2,1,0:T(8,128)(2,1)}, u32[]{:S(2)}) copy-start(bf16[1,2,4,48,1024]{4,3,2,1,0:T(8,128)(2,1)} %copy.47) | copy-start | bytes 2359300
  192.6 0.9 copy-start.16
  213.9 178.0 %reduce-scatter.11.cloned.1.call-start = ((), (), s32[]{:S(2)}) async-start(), calls=%async_computation.11 | async-start | bytes 4718592 | tf_op jit(solution)/shard_map/reduce_scatter | solution.py:123
  226.0 15.9 %all-to-all-start.3 = ((bf16[1,2,192,1024]{3,1,0,2:T(2,128)(2,1)}), bf16[1,2,192,1024]{3,1,0,2:T(2,128)(2,1)}, u32[]{:S(2)}, u32[]{:S(2)}) async-start(bf16[1,2,192,1024]{3,1,0,2:T(2,128)(2,1)} %copy.51), calls=%async_computation.3 | async-start | bytes 1572864 | tf_op jit(solution)/shard_map/all_to_all | solution.py:117
  241.9 15.9 %all-to-all-start.1 = ((bf16[1,2,192,1024]{3,1,0,2:T(2,128)(2,1)}), bf16[1,2,192,1024]{3,1,0,2:T(2,128)(2,1)}, u32[]{:S(2)}, u32[]{:S(2)}) async-start(bf16[1,2,192,1024]{3,1,0,2:T(2,128)(2,1)} %copy.48), calls=%async_computation.1 | async-start | bytes 1572864 | tf_op jit(solution)/shard_map/all_to_all | solution.py:106
  246.1 285.1 %reduce-scatter.9.cloned.1.call-start = ((), (), s32[]{:S(2)}) async-start(), calls=%async_computation.10 | async-start | bytes 2162688 | tf_op jit(solution)/shard_map/reduce_scatter | solution.py:134
  267.3 5.0 copy-start.15
  271.5 0.8 copy-start.1
  274.1 374.4 %reduce-scatter.7.cloned.1.call-start = ((), (), s32[]{:S(2)}) async-start(), calls=%async_computation.9 | async-start | bytes 6488064 | tf_op jit(solution)/shard_map/reduce_scatter | solution.py:133
  280.2 1.9 copy-start.8
  280.2 1.9 copy-start.12
  280.2 2.4 copy-start.9
  280.2 2.4 copy-start.18
  282.6 1.0 copy-start.20
  284.1 1.8 copy-start.5
  285.0 0.9 copy-start.11
  289.6 2.5 copy-start.2
  289.6 2.5 copy-start.6
Sparse Core Ops, SparseCore 0:
  10.2 138.2 all-gather.1
  214.1 86.0 reduce-scatter.12
  304.3 87.6 reduce-scatter.10
  394.6 136.5 reduce-scatter.8
  538.2 110.2 reduce-scatter.6
